TPU v7x, 512 devices: a whole 4x4x16 slice. The times are simulated.
512 devices in a mesh: pair: 8 (over z_hi, y), blk: 64 (over z_lo, x, core).
Axes of the slice: x: 4, y: 4, z: 16 (z_hi: 2, z_lo: 8; z = z_hi * 8 + z_lo), core: 2. Of those that a mesh axis runs over, the one named last changes fastest.
Arguments:
- amps: bfloat16 [8192, 80200], P(('blk', 'pair')), may hold values from -6 to 6
- ints: bfloat16 [1024, 80200], P('blk', 'pair'), may hold values from -0.015625 to 0.015625
- block_of: int32 [64], replicated, may hold values from 0 to 63, each once
- pair_rows: int32 [8192, 2], P(('blk', 'pair')), may hold values from 0 to 119
- occ_energy: float32 [120], replicated, may hold values from -2 to -0.5
- vir_pair_energy: float32 [1024], replicated, may hold values from 1 to 6
Outputs:
- new_amps: float32 [8192, 1024], P(('blk', 'pair'))
Inputs may be any that keep to these rules, and one draw needn't show every extreme that they name: `block_of`: each of 0 to 63 once.
All inputs are finite; a program needn't handle non-finite values.
Results may differ from a plain program's by a relative error of at most 0.0003.
Values may be sent and summed in bfloat16 or wider, within the bound.
A program may use at most 128 MiB of HBM per device.

v0:
```python
import jax
import jax.numpy as jnp
from jax import lax
from jax.sharding import PartitionSpec as P

NV = 400


def contract(weighted, slab_part):
    return lax.dot_general(
        weighted, slab_part, (((1,), (1,)), ((), ())), preferred_element_type=jnp.float32
    )


def per_device(amps, ints, block_of, pair_rows, occ_energy, vir_pair_energy):
    relaid = lax.all_to_all(amps, "pair", split_axis=1, concat_axis=0, tiled=True)
    shard_width = relaid.shape[1]
    column = lax.axis_index("pair") * shard_width + lax.broadcasted_iota(
        jnp.int32, (1, shard_width), 1
    )
    weighted = relaid * jnp.where(column < NV, 1.0, 2.0).astype(jnp.bfloat16)
    gathered = lax.all_gather(ints, "blk", axis=0, tiled=True)
    stored = contract(weighted, gathered)
    summed = lax.psum_scatter(stored, "pair", scatter_dimension=0, tiled=True)
    blocks = block_of.shape[0]
    height = summed.shape[0]
    grouped = summed.reshape(height, blocks, summed.shape[1] // blocks)
    ladder = jnp.zeros_like(grouped).at[:, block_of].set(grouped).reshape(height, summed.shape[1])
    levels = lax.broadcasted_iota(jnp.int32, (1, 1, occ_energy.shape[0]), 2)
    one_hot = (pair_rows[:, :, None] == levels).astype(jnp.float32)
    occupied = jnp.sum(one_hot * occ_energy[None, None, :], axis=(1, 2))
    denominator = vir_pair_energy[None, :] - occupied[:, None]
    return ladder / denominator


def solution(mesh):
    placed = (P(("blk", "pair"), None), P("blk", "pair"), P(), P(("blk", "pair"), None), P(), P())
    return jax.shard_map(
        per_device, mesh=mesh, in_specs=placed, out_specs=P(("blk", "pair"), None), check_vma=False
    )
```

profile of v0, /device:TPU:2, one launch (start us, length us, event | category | flops | bytes accessed | tf_op | source)
XLA Modules:
  0.0 403.6 jit_solution(10764181286795484275)
XLA Ops:
  6.5 0.0 all-gather.2.cloned.1.call-start
  6.5 0.7 all-gather.2.cloned.1.call-update
  7.3 4.8 %all_to_all.14 = bf16[16,8,10025]{2,1,0:T(8,128)(2,1)S(1)} reshape(bf16[16,80200]{1,0:T(8,128)(2,1)} %param.6) | data formatting | bytes 5132800 | tf_op jit(solution)/shard_map/all_to_all | solution.py:16
  12.1 1.8 copy.13
  13.9 17.7 %all-to-all-start = ((bf16[16,8,10025]{2,0,1:T(8,128)(2,1)}), bf16[16,8,10025]{2,0,1:T(8,128)(2,1)}, u32[]{:S(2)}, u32[]{:S(2)}) async-start(bf16[16,8,10025]{2,0,1:T(8,128)(2,1)} %copy.13), calls=%async_computation | async-start | bytes 5177344 | tf_op jit(solution)/shard_map/all_to_all | solution.py:16
  31.6 0.0 reduce-scatter.2.cloned.1.call-start
  31.7 66.3 %all-to-all-done = bf16[16,8,10025]{2,0,1:T(8,128)(2,1)} async-done(((bf16[16,8,10025]{2,0,1:T(8,128)(2,1)}), bf16[16,8,10025]{2,0,1:T(8,128)(2,1)}, u32[]{:S(2)}, u32[]{:S(2)}) %all-to-all-start) | async-done | bytes 2566432 | tf_op jit(solution)/shard_map/all_to_all | solution.py:16
  97.9 2.1 bitcast_multiply_fusion
  100.0 0.0 copy-start.1
  100.0 0.0 copy-start.2
  100.1 0.0 copy-start.3
  100.1 166.9 %all-gather.2.cloned.1.call-done = bf16[1024,10025]{1,0:T(8,128)(2,1)} async-done(((bf16[16,10025]{1,0:T(8,128)(2,1)}), bf16[1024,10025]{1,0:T(8,128)(2,1)}) %all-gather.2.cloned.1.call-update) | async-done | bytes 20531216 | tf_op jit(solution)/shard_map/all_gather | solution.py:22
  267.0 11.9 %fusion = f32[128,1024]{1,0:T(8,128)} fusion(bf16[128,10025]{1,0:T(8,128)(2,1)S(1)} %bitcast_multiply_fusion, bf16[1024,10025]{1,0:T(8,128)(2,1)} %all-gather.2.cloned.1.call-done), kind=kOutput, calls=%fused_computation.8 | convolution fusion | flops 2627993600 | bytes 23621888 | tf_op jit(solution)/shard_map/dot_general | solution.py:10
  278.8 0.0 reduce-scatter.2.cloned.1.call-update
  278.9 0.0 copy-done.1
  278.9 0.0 copy-done.2
  278.9 0.2 select_reduce_fusion
  279.1 0.0 copy-done.3
  279.1 0.0 copy-start
  279.1 112.7 %reduce-scatter.2.cloned.1.call-done = f32[16,1024]{1,0:T(8,128)} async-done(((f32[128,1024]{1,0:T(8,128)}), f32[16,1024]{1,0:T(8,128)}) %reduce-scatter.2.cloned.1.call-update) | async-done | bytes 65552 | tf_op jit(solution)/shard_map/reduce_scatter | solution.py:24
  391.8 1.0 reshape.27
  392.8 0.3 copy.14
  393.2 2.4 scatter_fusion
  395.6 0.2 copy.15
  395.8 0.3 reshape.25
  396.1 0.0 copy-done
  396.1 0.7 subtract_divide_fusion
  (3 shorter events, 0.1 us)
Async XLA Ops:
  6.5 260.4 %all-gather.2.cloned.1.call-start = ((), (), s32[]{:S(2)}) async-start(), calls=%async_computation.2 | async-start | bytes 21032960 | tf_op jit(solution)/shard_map/all_gather | solution.py:22
  13.9 84.1 %all-to-all-start = ((bf16[16,8,10025]{2,0,1:T(8,128)(2,1)}), bf16[16,8,10025]{2,0,1:T(8,128)(2,1)}, u32[]{:S(2)}, u32[]{:S(2)}) async-start(bf16[16,8,10025]{2,0,1:T(8,128)(2,1)} %copy.13), calls=%async_computation | async-start | bytes 5177344 | tf_op jit(solution)/shard_map/all_to_all | solution.py:16
  31.6 360.2 %reduce-scatter.2.cloned.1.call-start = ((), (), s32[]{:S(2)}) async-start(), calls=%async_computation.3 | async-start | bytes 589824 | tf_op jit(solution)/shard_map/reduce_scatter | solution.py:24
  100.0 178.8 %copy-start.1 = (s32[16,2]{0,1:T(2,128)S(1)}, s32[16,2]{0,1:T(2,128)}, u32[]{:S(2)}) copy-start(s32[16,2]{0,1:T(2,128)} %param.9) | copy-start | bytes 388
  100.0 178.8 %copy-start.2 = (f32[120]{0:T(128)S(1)}, f32[120]{0:T(128)}, u32[]{:S(2)}) copy-start(f32[120]{0:T(128)} %param.10) | copy-start | bytes 1444
  100.1 179.0 %copy-start.3 = (s32[64]{0:T(128)S(1)}, s32[64]{0:T(128)}, u32[]{:S(2)}) copy-start(s32[64]{0:T(128)} %param.8) | copy-start | bytes 772
  279.1 117.0 %copy-start = (f32[1024]{0:T(1024)S(1)}, f32[1024]{0:T(1024)}, u32[]{:S(2)}) copy-start(f32[1024]{0:T(1024)} %param.11) | copy-start | bytes 12292
Sparse Core Ops, SparseCore 0:
  9.5 257.4 all-gather.1
  279.0 112.7 reduce-scatter.1
where the time goes:
time: 404 us
  waiting for transfers between devices  347 us (86%)
  starting transfers between devices  17.8 us (4%)
  between operations  13.5 us (3%)
  matrix products  11.9 us (3%)
  local copies, waits for them, and re-layouts  10.9 us (3%)
    all_gather x1, waiting for transfers between devices, per_device(): gathered = lax.all_gather(ints, 'blk', axis=0, tiled=True)  167 us
    reduce_scatter x1, waiting for transfers between devices, per_device(): summed = lax.psum_scatter(stored, 'pair', scatter_dimension=0, tiled=True)  113 us
    all_to_all x1, waiting for transfers between devices, per_device(): lax.all_to_all(amps, 'pair', split_axis=1, concat_axis=0, tiled=True)  66.3 us
    all_to_all x1, starting transfers between devices, per_device(): lax.all_to_all(amps, 'pair', split_axis=1, concat_axis=0, tiled=True)  17.7 us
    dot_general x1, matrix products, contract(): lax.dot_general(weighted, slab_part, (((1,), (1,)), ((), ())), preferred_...  11.9 us
  transfers between devices with their start and end apart: 3, of which 3 were waited for; matrix products, arithmetic and copies ran while one was open for 1% of the time, Pallas kernels for 0%

commit v1 on v0

--- a/solution.py
+++ b/solution.py
@@ -19,7 +19,9 @@
         jnp.int32, (1, shard_width), 1
     )
     weighted = relaid * jnp.where(column < NV, 1.0, 2.0).astype(jnp.bfloat16)
-    gathered = lax.all_gather(ints, "blk", axis=0, tiled=True)
+    gathered = jnp.concatenate(
+        lax.all_to_all(jnp.stack([ints] * lax.axis_size("blk")), "blk", 0, 0), axis=0
+    )
     stored = contract(weighted, gathered)
     summed = lax.psum_scatter(stored, "pair", scatter_dimension=0, tiled=True)
     blocks = block_of.shape[0]

time: 404 us -> 1200 us (2.97)
  waiting for transfers between devices: 347 us -> 1000 us
  blocking collectives: 0 us -> 80.3 us
  starting transfers between devices: 17.8 us -> 70 us
    all_to_all x1, waiting for transfers between devices: 66.3 us -> 899 us  [per_device(): lax.all_to_all(jnp.stack([ints] * lax.axis_size('blk')), 'blk', 0, 0)]
    all_gather x1 -> x0, waiting for transfers between devices: 167 us -> none  [per_device(): gathered = lax.all_gather(ints, 'blk', axis=0, tiled=True)]
    all_to_all x0 -> x1, blocking collectives: none -> 80.3 us  [per_device(): lax.all_to_all(amps, 'pair', split_axis=1, concat_axis=0, tiled=True)]
    all_to_all x1, starting transfers between devices: 17.7 us -> 69.9 us  [per_device(): lax.all_to_all(jnp.stack([ints] * lax.axis_size('blk')), 'blk', 0, 0)]
  transfers between devices with their start and end apart: 3 -> 2, of which waited for: 3 -> 2; matrix products, arithmetic and copies ran while one was open for 1% -> 0% of each run, Pallas kernels for 0% -> 0%
where the time goes in v1:
time: 1200 us
  waiting for transfers between devices  1000 us (83%)
  blocking collectives  80.3 us (7%)
  starting transfers between devices  70 us (6%)
  local copies, waits for them, and re-layouts  16.5 us (1%)
  between operations  13.5 us (1%)
    all_to_all x1, waiting for transfers between devices, per_device(): lax.all_to_all(jnp.stack([ints] * lax.axis_size('blk')), 'blk', 0, 0)  899 us
    reduce_scatter x1, waiting for transfers between devices, per_device(): summed = lax.psum_scatter(stored, 'pair', scatter_dimension=0, tiled=True)  101 us
    all_to_all x1, blocking collectives, per_device(): lax.all_to_all(amps, 'pair', split_axis=1, concat_axis=0, tiled=True)  80.3 us
    all_to_all x1, starting transfers between devices, per_device(): lax.all_to_all(jnp.stack([ints] * lax.axis_size('blk')), 'blk', 0, 0)  69.9 us
  transfers between devices with their start and end apart: 2, of which 2 were waited for; matrix products, arithmetic and copies ran while one was open for 0% of the time, Pallas kernels for 0%

profile of v1, /device:TPU:2, one launch (start us, length us, event | category | flops | bytes accessed | tf_op | source)
XLA Modules:
  0.0 1195.7 jit_solution(2238124568183181606)
XLA Ops:
  6.5 4.8 all_to_all.13
  11.4 0.3 copy.13
  11.6 0.0 copy-start
  11.6 80.3 %all_to_all.18 = bf16[16,8,10025]{2,0,1:T(8,128)(2,1)} all-to-all(bf16[16,8,10025]{2,0,1:T(8,128)(2,1)S(1)} %copy.13), channel_id=1, replica_groups=mesh['pair'=8,'blk'=64] {'pair'}, dimensions={1} | all-to-all | bytes 5132800 | tf_op jit(solution)/shard_map/all_to_all | solution.py:16
  92.0 0.0 copy-done
  92.0 7.2 stack.2
  99.2 69.9 %all-to-all-start.1 = ((bf16[64,16,10025]{2,1,0:T(8,128)(2,1)}), bf16[64,16,10025]{2,1,0:T(8,128)(2,1)}, u32[]{:S(2)}, u32[]{:S(2)}) async-start(bf16[64,16,10025]{2,1,0:T(8,128)(2,1)} %stack.2), calls=%async_computation.1 | async-start | bytes 41418752 | tf_op jit(solution)/shard_map/all_to_all | solution.py:23
  169.1 0.0 reduce-scatter.2.cloned.1.call-start
  169.2 2.1 broadcast_multiply_fusion
  171.2 899.1 %all-to-all-done.1 = bf16[64,16,10025]{2,1,0:T(8,128)(2,1)} async-done(((bf16[64,16,10025]{2,1,0:T(8,128)(2,1)}), bf16[64,16,10025]{2,1,0:T(8,128)(2,1)}, u32[]{:S(2)}, u32[]{:S(2)}) %all-to-all-start.1) | async-done | bytes 20531232 | tf_op jit(solution)/shard_map/all_to_all | solution.py:23
  1070.4 0.0 copy-start.2
  1070.4 0.0 copy-start.3
  1070.4 0.0 copy-start.4
  1070.4 11.9 fusion
  1082.3 0.0 reduce-scatter.2.cloned.1.call-update
  1082.3 0.0 copy-done.2
  1082.3 0.0 copy-done.3
  1082.3 0.2 select_reduce_fusion
  1082.5 0.0 copy-done.4
  1082.5 0.0 copy-start.1
  1082.5 101.3 %reduce-scatter.2.cloned.1.call-done = f32[16,1024]{1,0:T(8,128)} async-done(((f32[128,1024]{1,0:T(8,128)}), f32[16,1024]{1,0:T(8,128)}) %reduce-scatter.2.cloned.1.call-update) | async-done | bytes 65552 | tf_op jit(solution)/shard_map/reduce_scatter | solution.py:26
  1183.8 1.0 reshape.39
  1184.9 0.3 copy.14
  1185.2 2.4 scatter_fusion
  1187.7 0.2 copy.15
  1187.8 0.3 reshape.37
  1188.1 0.0 copy-done.1
  1188.1 0.7 subtract_divide_fusion
  (3 shorter events, 0.1 us)
Async XLA Ops:
  11.6 80.3 %copy-start = (bf16[16,10025]{1,0:T(8,128)(2,1)S(1)}, bf16[16,10025]{1,0:T(8,128)(2,1)}, u32[]{:S(2)}) copy-start(bf16[16,10025]{1,0:T(8,128)(2,1)} %param.7) | copy-start | bytes 962404
  99.2 971.2 %all-to-all-start.1 = ((bf16[64,16,10025]{2,1,0:T(8,128)(2,1)}), bf16[64,16,10025]{2,1,0:T(8,128)(2,1)}, u32[]{:S(2)}, u32[]{:S(2)}) async-start(bf16[64,16,10025]{2,1,0:T(8,128)(2,1)} %stack.2), calls=%async_computation.1 | async-start | bytes 41418752 | tf_op jit(solution)/shard_map/all_to_all | solution.py:23
  169.1 1014.7 %reduce-scatter.2.cloned.1.call-start = ((), (), s32[]{:S(2)}) async-start(), calls=%async_computation.3 | async-start | bytes 589824 | tf_op jit(solution)/shard_map/reduce_scatter | solution.py:26
  1070.4 12.0 copy-start.2
  1070.4 12.0 %copy-start.3 = (f32[120]{0:T(128)S(1)}, f32[120]{0:T(128)}, u32[]{:S(2)}) copy-start(f32[120]{0:T(128)} %param.10) | copy-start | bytes 1444
  1070.4 12.2 %copy-start.4 = (s32[64]{0:T(128)S(1)}, s32[64]{0:T(128)}, u32[]{:S(2)}) copy-start(s32[64]{0:T(128)} %param.8) | copy-start | bytes 772
  1082.5 105.6 %copy-start.1 = (f32[1024]{0:T(1024)S(1)}, f32[1024]{0:T(1024)}, u32[]{:S(2)}) copy-start(f32[1024]{0:T(1024)} %param.11) | copy-start | bytes 12292
Sparse Core Ops, SparseCore 0:
  1082.4 101.3 reduce-scatter.1
